TPU v7x, 32 devices: a whole 2x2x4 slice. The times are simulated.
32 devices in a mesh: blk: 16 (over z, y, x), grp: 2 (over core).
Axes of the slice: x: 2, y: 2, z: 4, core: 2. Of those that a mesh axis runs over, the one named last changes fastest.
Arguments:
- x_blocks: bfloat16 [512, 128, 128], P(('blk', 'grp')), may hold values from -0.59765625 to 0.59765625
- pair_left: int32 [16, 2, 16, 12], P('blk', 'grp'), may hold values from 0 to 31
- pair_right: int32 [16, 2, 16, 12], P('blk', 'grp'), may hold values from 0 to 31
- pair_target: int32 [16, 2, 16, 12], P('blk', 'grp'), may hold values from 0 to 3
Outputs:
- c_blocks: bfloat16 [16, 2, 4, 128, 128], P('blk', 'grp')
All inputs are finite; a program needn't handle non-finite values.
Results may differ from a plain program's by a relative error of at most 0.001.
Values may be sent and summed in bfloat16 or wider, within the bound.
A program may use at most 64 MiB of HBM per device.

v0:
```python
import jax
import jax.numpy as jnp
from jax import lax
from jax.sharding import PartitionSpec as P

CS = 4


def from_behind(block, axis, distance):
    devices = range(lax.axis_size(axis))
    route = [((i - distance) % len(devices), i) for i in devices]
    return lax.ppermute(block, axis, route)


def per_device(x_blocks, pair_left, pair_right, pair_target):
    gathered = lax.all_gather(x_blocks, "grp", axis=0, tiled=True)
    group_count = lax.axis_size("blk")
    left_all = pair_left[0, 0]
    right_all = pair_right[0, 0]
    target_all = pair_target[0, 0]
    block_order = x_blocks.shape[1]
    panel_count = gathered.shape[0]
    pair_count = left_all.shape[1]
    flat_panel = gathered.reshape(panel_count, block_order * block_order)

    def partial_value(turn_index):
        left_index = lax.dynamic_index_in_dim(left_all, turn_index, 0, keepdims=False)
        right_index = lax.dynamic_index_in_dim(right_all, turn_index, 0, keepdims=False)
        target_index = lax.dynamic_index_in_dim(target_all, turn_index, 0, keepdims=False)
        both_index = jnp.concatenate([left_index, right_index])
        one_hot = (both_index[:, None] == jnp.arange(panel_count, dtype=jnp.int32)[None, :]).astype(
            jnp.bfloat16
        )
        picked = jnp.dot(one_hot, flat_panel, preferred_element_type=jnp.float32).astype(
            jnp.bfloat16
        )
        picked = picked.reshape(2 * pair_count, block_order, block_order)
        left_tiles = picked[:pair_count]
        right_tiles = picked[pair_count:]
        product = jnp.einsum(
            "pxy,pxz->pyz", left_tiles, right_tiles, preferred_element_type=jnp.float32
        )
        selector = (target_index[:, None] == jnp.arange(CS, dtype=jnp.int32)[None, :]).astype(
            jnp.float32
        )
        return jnp.einsum("pc,pyz->cyz", selector, product, precision=lax.Precision.HIGHEST)

    def advance(turn_index, carried):
        arrived = from_behind(carried, "blk", 1)
        return arrived + partial_value(turn_index)

    summed = lax.fori_loop(1, group_count, advance, partial_value(0))
    return summed.astype(jnp.bfloat16).reshape(1, 1, CS, block_order, block_order)


def solution(mesh):
    return jax.shard_map(
        per_device,
        mesh=mesh,
        in_specs=(
            P(("blk", "grp"), None, None),
            P("blk", "grp", None, None),
            P("blk", "grp", None, None),
            P("blk", "grp", None, None),
        ),
        out_specs=P("blk", "grp", None, None, None),
        check_vma=False,
    )
```

profile of v0, /device:TPU:0, one launch (start us, length us, event | category | flops | bytes accessed | tf_op | source)
XLA Modules:
  0.0 208.5 jit_solution(14944248637983709933)
XLA Ops:
  6.5 0.7 all-gather.2.cloned.1.call-update
  7.3 0.8 copy.18
  8.0 0.8 copy.19
  8.8 0.8 copy.17
  9.6 1.2 slice_reduce_fusion
  10.9 1.0 slice_reduce_fusion.2
  11.9 8.8 %all-gather.2.cloned.1.call-done = bf16[32,128,128]{2,1,0:T(8,128)(2,1)} async-done(((bf16[16,128,128]{2,1,0:T(8,128)(2,1)}), bf16[32,128,128]{2,1,0:T(8,128)(2,1)}) %all-gather.2.cloned.1.call-update) | async-done | bytes 1048592 | tf_op jit(solution)/shard_map/all_gather | solution.py:16
  20.7 2.0 copy.37
  22.7 0.7 convolution_convert_fusion.1
  24.0 0.9 fusion.11
  25.0 176.0 %while.15 = (s32[]{:T(128)}, f32[4,128,128]{2,0,1:T(4,128)S(1)}, s32[16,12]{1,0:T(8,128)S(1)}, s32[16,12]{1,0:T(8,128)S(1)}, s32[16,12]{1,0:T(8,128)S(1)}, /*ind...) while((s32[]{:T(128)}, f32[4,128,128]{2,0,1:T(4,128)S(1)}, s32[16,12]{1,0:T(8,128)S(1)}, ...), condition=%wide.region_1.2_spmd, body=%wide.region_0.1_spmd.sunk | while | flops 85394256 | bytes 9437983 | solution.py:52
  25.0 1.8 collective-permute-start
  27.9 9.3 %collective-permute-done = f32[4,128,128]{2,0,1:T(4,128)S(1)} collective-permute-done((f32[4,128,128]{2,0,1:T(4,128)S(1)}, f32[4,128,128]{2,0,1:T(4,128)S(1)}, u32[]{:S(2)}, u32[]{:S(2)}) %collective-permute-start) | collective-permute-done | bytes 262176 | tf_op jit(solution)/shard_map/while/body/eval_jaxpr/ppermute | solution.py:12
  37.2 0.9 convolution_add_fusion.2
  39.4 10.2 %collective-permute-done = f32[4,128,128]{2,0,1:T(4,128)S(1)} collective-permute-done((f32[4,128,128]{2,0,1:T(4,128)S(1)}, f32[4,128,128]{2,0,1:T(4,128)S(1)}, u32[]{:S(2)}, u32[]{:S(2)}) %collective-permute-start) | collective-permute-done | bytes 262176 | tf_op jit(solution)/shard_map/while/body/eval_jaxpr/ppermute | solution.py:12
  49.5 0.9 convolution_add_fusion.2
  50.7 0.4 convolution_convert_fusion.3
  51.7 9.3 %collective-permute-done = f32[4,128,128]{2,0,1:T(4,128)S(1)} collective-permute-done((f32[4,128,128]{2,0,1:T(4,128)S(1)}, f32[4,128,128]{2,0,1:T(4,128)S(1)}, u32[]{:S(2)}, u32[]{:S(2)}) %collective-permute-start) | collective-permute-done | bytes 262176 | tf_op jit(solution)/shard_map/while/body/eval_jaxpr/ppermute | solution.py:12
  61.0 0.9 convolution_add_fusion.2
  63.2 8.8 %collective-permute-done = f32[4,128,128]{2,0,1:T(4,128)S(1)} collective-permute-done((f32[4,128,128]{2,0,1:T(4,128)S(1)}, f32[4,128,128]{2,0,1:T(4,128)S(1)}, u32[]{:S(2)}, u32[]{:S(2)}) %collective-permute-start) | collective-permute-done | bytes 262176 | tf_op jit(solution)/shard_map/while/body/eval_jaxpr/ppermute | solution.py:12
  71.9 0.9 convolution_add_fusion.2
  74.1 8.8 %collective-permute-done = f32[4,128,128]{2,0,1:T(4,128)S(1)} collective-permute-done((f32[4,128,128]{2,0,1:T(4,128)S(1)}, f32[4,128,128]{2,0,1:T(4,128)S(1)}, u32[]{:S(2)}, u32[]{:S(2)}) %collective-permute-start) | collective-permute-done | bytes 262176 | tf_op jit(solution)/shard_map/while/body/eval_jaxpr/ppermute | solution.py:12
  82.9 0.9 convolution_add_fusion.2
  84.0 0.4 convolution_convert_fusion.3
  85.1 8.8 %collective-permute-done = f32[4,128,128]{2,0,1:T(4,128)S(1)} collective-permute-done((f32[4,128,128]{2,0,1:T(4,128)S(1)}, f32[4,128,128]{2,0,1:T(4,128)S(1)}, u32[]{:S(2)}, u32[]{:S(2)}) %collective-permute-start) | collective-permute-done | bytes 262176 | tf_op jit(solution)/shard_map/while/body/eval_jaxpr/ppermute | solution.py:12
  93.8 0.9 convolution_add_fusion.2
  96.0 8.8 %collective-permute-done = f32[4,128,128]{2,0,1:T(4,128)S(1)} collective-permute-done((f32[4,128,128]{2,0,1:T(4,128)S(1)}, f32[4,128,128]{2,0,1:T(4,128)S(1)}, u32[]{:S(2)}, u32[]{:S(2)}) %collective-permute-start) | collective-permute-done | bytes 262176 | tf_op jit(solution)/shard_map/while/body/eval_jaxpr/ppermute | solution.py:12
  104.8 0.9 convolution_add_fusion.2
  107.0 9.5 %collective-permute-done = f32[4,128,128]{2,0,1:T(4,128)S(1)} collective-permute-done((f32[4,128,128]{2,0,1:T(4,128)S(1)}, f32[4,128,128]{2,0,1:T(4,128)S(1)}, u32[]{:S(2)}, u32[]{:S(2)}) %collective-permute-start) | collective-permute-done | bytes 262176 | tf_op jit(solution)/shard_map/while/body/eval_jaxpr/ppermute | solution.py:12
  116.5 0.9 convolution_add_fusion.2
  117.6 0.4 convolution_convert_fusion.3
  118.7 10.7 %collective-permute-done = f32[4,128,128]{2,0,1:T(4,128)S(1)} collective-permute-done((f32[4,128,128]{2,0,1:T(4,128)S(1)}, f32[4,128,128]{2,0,1:T(4,128)S(1)}, u32[]{:S(2)}, u32[]{:S(2)}) %collective-permute-start) | collective-permute-done | bytes 262176 | tf_op jit(solution)/shard_map/while/body/eval_jaxpr/ppermute | solution.py:12
  129.4 0.9 convolution_add_fusion.2
  130.5 0.4 convolution_convert_fusion.3
  131.5 11.3 %collective-permute-done = f32[4,128,128]{2,0,1:T(4,128)S(1)} collective-permute-done((f32[4,128,128]{2,0,1:T(4,128)S(1)}, f32[4,128,128]{2,0,1:T(4,128)S(1)}, u32[]{:S(2)}, u32[]{:S(2)}) %collective-permute-start) | collective-permute-done | bytes 262176 | tf_op jit(solution)/shard_map/while/body/eval_jaxpr/ppermute | solution.py:12
  142.8 0.9 convolution_add_fusion.2
  145.0 10.4 %collective-permute-done = f32[4,128,128]{2,0,1:T(4,128)S(1)} collective-permute-done((f32[4,128,128]{2,0,1:T(4,128)S(1)}, f32[4,128,128]{2,0,1:T(4,128)S(1)}, u32[]{:S(2)}, u32[]{:S(2)}) %collective-permute-start) | collective-permute-done | bytes 262176 | tf_op jit(solution)/shard_map/while/body/eval_jaxpr/ppermute | solution.py:12
  155.5 0.9 convolution_add_fusion.2
  156.6 0.4 convolution_convert_fusion.3
  157.6 9.6 %collective-permute-done = f32[4,128,128]{2,0,1:T(4,128)S(1)} collective-permute-done((f32[4,128,128]{2,0,1:T(4,128)S(1)}, f32[4,128,128]{2,0,1:T(4,128)S(1)}, u32[]{:S(2)}, u32[]{:S(2)}) %collective-permute-start) | collective-permute-done | bytes 262176 | tf_op jit(solution)/shard_map/while/body/eval_jaxpr/ppermute | solution.py:12
  167.2 0.9 convolution_add_fusion.2
  169.4 8.8 %collective-permute-done = f32[4,128,128]{2,0,1:T(4,128)S(1)} collective-permute-done((f32[4,128,128]{2,0,1:T(4,128)S(1)}, f32[4,128,128]{2,0,1:T(4,128)S(1)}, u32[]{:S(2)}, u32[]{:S(2)}) %collective-permute-start) | collective-permute-done | bytes 262176 | tf_op jit(solution)/shard_map/while/body/eval_jaxpr/ppermute | solution.py:12
  178.1 0.9 convolution_add_fusion.2
  180.3 8.8 %collective-permute-done = f32[4,128,128]{2,0,1:T(4,128)S(1)} collective-permute-done((f32[4,128,128]{2,0,1:T(4,128)S(1)}, f32[4,128,128]{2,0,1:T(4,128)S(1)}, u32[]{:S(2)}, u32[]{:S(2)}) %collective-permute-start) | collective-permute-done | bytes 262176 | tf_op jit(solution)/shard_map/while/body/eval_jaxpr/ppermute | solution.py:12
  189.1 0.9 convolution_add_fusion.2
  191.3 8.8 %collective-permute-done = f32[4,128,128]{2,0,1:T(4,128)S(1)} collective-permute-done((f32[4,128,128]{2,0,1:T(4,128)S(1)}, f32[4,128,128]{2,0,1:T(4,128)S(1)}, u32[]{:S(2)}, u32[]{:S(2)}) %collective-permute-start) | collective-permute-done | bytes 262176 | tf_op jit(solution)/shard_map/while/body/eval_jaxpr/ppermute | solution.py:12
  200.0 0.9 convolution_add_fusion.2
  201.0 0.7 copy.38
  (137 shorter events, 16.5 us)
Async XLA Ops:
  6.5 14.1 %all-gather.2.cloned.1.call-start = ((), (), s32[]{:S(2)}) async-start(), calls=%async_computation | async-start | bytes 1572864 | tf_op jit(solution)/shard_map/all_gather | solution.py:16
  20.7 2.0 copy-start
  25.0 12.2 %collective-permute-start = (f32[4,128,128]{2,0,1:T(4,128)S(1)}, f32[4,128,128]{2,0,1:T(4,128)S(1)}, u32[]{:S(2)}, u32[]{:S(2)}) collective-permute-start(f32[4,128,128]{2,0,1:T(4,128)S(1)} %get-tuple-element.235), channel_id=1, source_target_pairs={{30,0},{0,2},{2,4},{4,6},{6,8},{8,10},{10,12},{12,14},{14,16},{16,... | collective-permute-start | bytes 786440 | tf_op jit(solution)/shard_map/while/body/eval_jaxpr/ppermute | solution.py:12
  38.1 11.4 %collective-permute-start = (f32[4,128,128]{2,0,1:T(4,128)S(1)}, f32[4,128,128]{2,0,1:T(4,128)S(1)}, u32[]{:S(2)}, u32[]{:S(2)}) collective-permute-start(f32[4,128,128]{2,0,1:T(4,128)S(1)} %get-tuple-element.235), channel_id=1, source_target_pairs={{30,0},{0,2},{2,4},{4,6},{6,8},{8,10},{10,12},{12,14},{14,16},{16,... | collective-permute-start | bytes 786440 | tf_op jit(solution)/shard_map/while/body/eval_jaxpr/ppermute | solution.py:12
  50.5 10.5 %collective-permute-start = (f32[4,128,128]{2,0,1:T(4,128)S(1)}, f32[4,128,128]{2,0,1:T(4,128)S(1)}, u32[]{:S(2)}, u32[]{:S(2)}) collective-permute-start(f32[4,128,128]{2,0,1:T(4,128)S(1)} %get-tuple-element.235), channel_id=1, source_target_pairs={{30,0},{0,2},{2,4},{4,6},{6,8},{8,10},{10,12},{12,14},{14,16},{16,... | collective-permute-start | bytes 786440 | tf_op jit(solution)/shard_map/while/body/eval_jaxpr/ppermute | solution.py:12
  61.9 10.0 %collective-permute-start = (f32[4,128,128]{2,0,1:T(4,128)S(1)}, f32[4,128,128]{2,0,1:T(4,128)S(1)}, u32[]{:S(2)}, u32[]{:S(2)}) collective-permute-start(f32[4,128,128]{2,0,1:T(4,128)S(1)} %get-tuple-element.235), channel_id=1, source_target_pairs={{30,0},{0,2},{2,4},{4,6},{6,8},{8,10},{10,12},{12,14},{14,16},{16,... | collective-permute-start | bytes 786440 | tf_op jit(solution)/shard_map/while/body/eval_jaxpr/ppermute | solution.py:12
  72.9 10.0 %collective-permute-start = (f32[4,128,128]{2,0,1:T(4,128)S(1)}, f32[4,128,128]{2,0,1:T(4,128)S(1)}, u32[]{:S(2)}, u32[]{:S(2)}) collective-permute-start(f32[4,128,128]{2,0,1:T(4,128)S(1)} %get-tuple-element.235), channel_id=1, source_target_pairs={{30,0},{0,2},{2,4},{4,6},{6,8},{8,10},{10,12},{12,14},{14,16},{16,... | collective-permute-start | bytes 786440 | tf_op jit(solution)/shard_map/while/body/eval_jaxpr/ppermute | solution.py:12
  83.8 10.0 %collective-permute-start = (f32[4,128,128]{2,0,1:T(4,128)S(1)}, f32[4,128,128]{2,0,1:T(4,128)S(1)}, u32[]{:S(2)}, u32[]{:S(2)}) collective-permute-start(f32[4,128,128]{2,0,1:T(4,128)S(1)} %get-tuple-element.235), channel_id=1, source_target_pairs={{30,0},{0,2},{2,4},{4,6},{6,8},{8,10},{10,12},{12,14},{14,16},{16,... | collective-permute-start | bytes 786440 | tf_op jit(solution)/shard_map/while/body/eval_jaxpr/ppermute | solution.py:12
  94.7 10.0 %collective-permute-start = (f32[4,128,128]{2,0,1:T(4,128)S(1)}, f32[4,128,128]{2,0,1:T(4,128)S(1)}, u32[]{:S(2)}, u32[]{:S(2)}) collective-permute-start(f32[4,128,128]{2,0,1:T(4,128)S(1)} %get-tuple-element.235), channel_id=1, source_target_pairs={{30,0},{0,2},{2,4},{4,6},{6,8},{8,10},{10,12},{12,14},{14,16},{16,... | collective-permute-start | bytes 786440 | tf_op jit(solution)/shard_map/while/body/eval_jaxpr/ppermute | solution.py:12
  105.7 10.8 %collective-permute-start = (f32[4,128,128]{2,0,1:T(4,128)S(1)}, f32[4,128,128]{2,0,1:T(4,128)S(1)}, u32[]{:S(2)}, u32[]{:S(2)}) collective-permute-start(f32[4,128,128]{2,0,1:T(4,128)S(1)} %get-tuple-element.235), channel_id=1, source_target_pairs={{30,0},{0,2},{2,4},{4,6},{6,8},{8,10},{10,12},{12,14},{14,16},{16,... | collective-permute-start | bytes 786440 | tf_op jit(solution)/shard_map/while/body/eval_jaxpr/ppermute | solution.py:12
  117.4 12.0 %collective-permute-start = (f32[4,128,128]{2,0,1:T(4,128)S(1)}, f32[4,128,128]{2,0,1:T(4,128)S(1)}, u32[]{:S(2)}, u32[]{:S(2)}) collective-permute-start(f32[4,128,128]{2,0,1:T(4,128)S(1)} %get-tuple-element.235), channel_id=1, source_target_pairs={{30,0},{0,2},{2,4},{4,6},{6,8},{8,10},{10,12},{12,14},{14,16},{16,... | collective-permute-start | bytes 786440 | tf_op jit(solution)/shard_map/while/body/eval_jaxpr/ppermute | solution.py:12
  130.3 12.6 %collective-permute-start = (f32[4,128,128]{2,0,1:T(4,128)S(1)}, f32[4,128,128]{2,0,1:T(4,128)S(1)}, u32[]{:S(2)}, u32[]{:S(2)}) collective-permute-start(f32[4,128,128]{2,0,1:T(4,128)S(1)} %get-tuple-element.235), channel_id=1, source_target_pairs={{30,0},{0,2},{2,4},{4,6},{6,8},{8,10},{10,12},{12,14},{14,16},{16,... | collective-permute-start | bytes 786440 | tf_op jit(solution)/shard_map/while/body/eval_jaxpr/ppermute | solution.py:12
  143.8 11.7 %collective-permute-start = (f32[4,128,128]{2,0,1:T(4,128)S(1)}, f32[4,128,128]{2,0,1:T(4,128)S(1)}, u32[]{:S(2)}, u32[]{:S(2)}) collective-permute-start(f32[4,128,128]{2,0,1:T(4,128)S(1)} %get-tuple-element.235), channel_id=1, source_target_pairs={{30,0},{0,2},{2,4},{4,6},{6,8},{8,10},{10,12},{12,14},{14,16},{16,... | collective-permute-start | bytes 786440 | tf_op jit(solution)/shard_map/while/body/eval_jaxpr/ppermute | solution.py:12
  156.4 10.8 %collective-permute-start = (f32[4,128,128]{2,0,1:T(4,128)S(1)}, f32[4,128,128]{2,0,1:T(4,128)S(1)}, u32[]{:S(2)}, u32[]{:S(2)}) collective-permute-start(f32[4,128,128]{2,0,1:T(4,128)S(1)} %get-tuple-element.235), channel_id=1, source_target_pairs={{30,0},{0,2},{2,4},{4,6},{6,8},{8,10},{10,12},{12,14},{14,16},{16,... | collective-permute-start | bytes 786440 | tf_op jit(solution)/shard_map/while/body/eval_jaxpr/ppermute | solution.py:12
  168.1 10.0 %collective-permute-start = (f32[4,128,128]{2,0,1:T(4,128)S(1)}, f32[4,128,128]{2,0,1:T(4,128)S(1)}, u32[]{:S(2)}, u32[]{:S(2)}) collective-permute-start(f32[4,128,128]{2,0,1:T(4,128)S(1)} %get-tuple-element.235), channel_id=1, source_target_pairs={{30,0},{0,2},{2,4},{4,6},{6,8},{8,10},{10,12},{12,14},{14,16},{16,... | collective-permute-start | bytes 786440 | tf_op jit(solution)/shard_map/while/body/eval_jaxpr/ppermute | solution.py:12
  179.1 10.0 %collective-permute-start = (f32[4,128,128]{2,0,1:T(4,128)S(1)}, f32[4,128,128]{2,0,1:T(4,128)S(1)}, u32[]{:S(2)}, u32[]{:S(2)}) collective-permute-start(f32[4,128,128]{2,0,1:T(4,128)S(1)} %get-tuple-element.235), channel_id=1, source_target_pairs={{30,0},{0,2},{2,4},{4,6},{6,8},{8,10},{10,12},{12,14},{14,16},{16,... | collective-permute-start | bytes 786440 | tf_op jit(solution)/shard_map/while/body/eval_jaxpr/ppermute | solution.py:12
  190.0 10.0 %collective-permute-start = (f32[4,128,128]{2,0,1:T(4,128)S(1)}, f32[4,128,128]{2,0,1:T(4,128)S(1)}, u32[]{:S(2)}, u32[]{:S(2)}) collective-permute-start(f32[4,128,128]{2,0,1:T(4,128)S(1)} %get-tuple-element.235), channel_id=1, source_target_pairs={{30,0},{0,2},{2,4},{4,6},{6,8},{8,10},{10,12},{12,14},{14,16},{16,... | collective-permute-start | bytes 786440 | tf_op jit(solution)/shard_map/while/body/eval_jaxpr/ppermute | solution.py:12
Sparse Core Ops, SparseCore 0:
  8.9 11.7 all-gather.1
where the time goes:
time: 209 us; the launch traced here: 208 us
  waiting for transfers between devices  151 us (72%)
  matrix products  26.5 us (13%)
  between operations  13.4 us (6%)
  local copies, waits for them, and re-layouts  12.4 us (6%)
  starting transfers between devices  2.59 us (1%)
    ppermute x15, waiting for transfers between devices, from_behind(): return lax.ppermute(block, axis, route)  142 us
    dot_general x16, matrix products, partial_value(): jnp.einsum('pc,pyz->cyz', selector, product, precision=lax.Precision.HIGH...  14.5 us
    all_gather x1, waiting for transfers between devices, per_device(): gathered = lax.all_gather(x_blocks, 'grp', axis=0, tiled=True)  8.79 us
    dot_general x16, matrix products, partial_value(): jnp.dot(one_hot, flat_panel, preferred_element_type=jnp.float32)  7.05 us
    dot_general x16, matrix products, partial_value(): jnp.einsum('pxy,pxz->pyz', left_tiles, right_tiles, preferred_element_typ...  5.03 us
    unnamed x8, local copies, waits for them, and re-layouts  4.48 us
  transfers between devices with their start and end apart: 16, of which 16 were waited for; matrix products, arithmetic and copies ran while one was open for 10% of the time, Pallas kernels for 0%

commit v1 on v0

v1 whole, which is shorter than its diff:
```python
import functools

import jax
import jax.numpy as jnp
from jax import lax
from jax.experimental import pallas as pl
from jax.experimental.pallas import tpu as pltpu
from jax.sharding import PartitionSpec as P

CS = 4
PLANE = 4
STEPS = 32700.0
FINE = 64.0
MESH = pl.DeviceIdType.MESH


def kernel(
    n, g, nb, bs, pairs,
    x_ref, left_ref, right_ref, target_ref, out_ref,
    panel, panel_t, prods, part, own, send1, recv1, send2, recv2,
    gather_send, gather_recv, sem_s1, sem_r1, sem_s2, sem_r2,
):
    planes = n // PLANE
    me = lax.axis_index("blk")
    q = lax.axis_index("grp")
    hi, lo = me // PLANE, me % PLANE
    body_rows = CS * bs

    def far(k):
        return (hi ^ k) * PLANE + lo

    def near(j):
        return hi * PLANE + (lo ^ j)

    barrier = pltpu.get_barrier_semaphore()
    for d in range(1, g):
        pl.semaphore_signal(barrier, inc=1, device_id=(me, (q + d) % g), device_id_type=MESH)
    for j in range(1, PLANE):
        pl.semaphore_signal(barrier, inc=1, device_id=(near(j), q), device_id_type=MESH)
    for k in range(1, planes):
        pl.semaphore_signal(barrier, inc=1, device_id=(far(k), q), device_id_type=MESH)
    pl.semaphore_wait(barrier, (g - 1) + (PLANE - 1) + (planes - 1))

    gathers = []
    for d in range(1, g):
        copy = pltpu.make_async_remote_copy(
            src_ref=x_ref,
            dst_ref=panel.at[pl.ds(q * nb, nb)],
            send_sem=gather_send.at[d - 1],
            recv_sem=gather_recv.at[d - 1],
            device_id=(me, (q + d) % g),
            device_id_type=MESH,
        )
        copy.start()
        gathers.append(copy)

    def take_own(i, _):
        block = x_ref[i]
        panel[q * nb + i] = block
        panel_t[q * nb + i] = block.T
        return 0

    lax.fori_loop(0, nb, take_own, 0)
    for d in range(1, g):
        gathers[d - 1].wait_recv()
        source = (q - d + g) % g

        def take_other(i, _):
            panel_t[source * nb + i] = panel[source * nb + i].T
            return 0

        lax.fori_loop(0, nb, take_other, 0)

    def partial_sum(owner, put):
        s = (me - 1 - owner + 2 * n) % n
        for p in range(pairs):
            prods[p] = jnp.dot(
                panel_t[left_ref[s, p]],
                panel[right_ref[s, p]],
                preferred_element_type=jnp.float32,
            )
        masks = [
            [jnp.where(target_ref[s, p] == c, 1.0, 0.0) for c in range(CS)] for p in range(pairs)
        ]
        strip = 16
        for i in range(bs // strip):
            rows = pl.ds(i * strip, strip)
            totals = [None] * CS
            for p in range(pairs):
                value = prods[p, rows, :]
                for c in range(CS):
                    term = value * masks[p][c]
                    totals[c] = term if totals[c] is None else totals[c] + term
            for c in range(CS):
                put(c, rows, totals[c])

    def encode(c, value, dst):
        most = jnp.max(jnp.abs(value), axis=0, keepdims=True)
        level = jnp.ceil(jnp.log(jnp.maximum(most, 1e-30)) * FINE) + 1.0
        inverse = jnp.exp(level * (-1.0 / FINE)) * STEPS
        coded = jnp.round(value * inverse).astype(jnp.int32).astype(jnp.int16)
        dst[pl.ds(c * bs, bs), :] = coded
        return level

    def put_levels(levels, dst):
        row = lax.broadcasted_iota(jnp.int32, (16, bs), 0)
        table = jnp.zeros((16, bs), jnp.float32)
        for c in range(CS):
            table = jnp.where(row == c, levels[c], table)
        dst[pl.ds(body_rows, 16), :] = table.astype(jnp.int32).astype(jnp.int16)

    def get_scales(src):
        level = src[pl.ds(body_rows, 16), :].astype(jnp.int32).astype(jnp.float32)
        return jnp.exp(level * (1.0 / FINE)) * (1.0 / STEPS)

    def decode(c, scales, src):
        value = src[pl.ds(c * bs, bs), :].astype(jnp.int32).astype(jnp.float32)
        return value * scales[c : c + 1, :]

    def copy1(t, j):
        return pltpu.make_async_remote_copy(
            src_ref=send1.at[t, j - 1],
            dst_ref=recv1.at[t, j - 1],
            send_sem=sem_s1.at[t, j - 1],
            recv_sem=sem_r1.at[t, j - 1],
            device_id=(near(j), q),
            device_id_type=MESH,
        )

    def copy2(t):
        return pltpu.make_async_remote_copy(
            src_ref=send2.at[t],
            dst_ref=recv2.at[t],
            send_sem=sem_s2.at[t],
            recv_sem=sem_r2.at[t],
            device_id=(far(t + 1), q),
            device_id_type=MESH,
        )

    def compute(t):
        base = (hi ^ ((t + 1) % planes)) * PLANE

        def put_part(c, rows, value):
            part[c, rows, :] = value

        def one(j, _):
            partial_sum(base + (lo ^ j), put_part)
            dst = send1.at[t, j - 1]
            put_levels([encode(c, part[c], dst) for c in range(CS)], dst)
            copy1(t, j).start()
            return 0

        lax.fori_loop(1, PLANE, one, 0)

        def put_own(c, rows, value):
            own[t, c, rows, :] = value

        partial_sum(base + lo, put_own)

    def plane_total(t):
        for j in range(1, PLANE):
            copy1(t, j).wait_recv()
        scales = [get_scales(recv1.at[t, j]) for j in range(PLANE - 1)]
        for c in range(CS):
            value = own[t, c]
            for j in range(PLANE - 1):
                value = value + decode(c, scales[j], recv1.at[t, j])
            yield c, value

    def pass_on(t):
        dst = send2.at[t]
        put_levels([encode(c, value, dst) for c, value in plane_total(t)], dst)
        copy2(t).start()

    lag = 2

    def turn(t, _):
        @pl.when(t < planes)
        def _():
            compute(t)

        @pl.when(t >= lag)
        def _():
            pass_on(t - lag)

        return 0

    lax.fori_loop(0, planes - 1 + lag, turn, 0)

    last = planes - 1
    totals = [value for _, value in plane_total(last)]
    for c in range(CS):
        own[last, c] = totals[c]
    for t in range(last):
        copy2(t).wait_recv()
    scales = [get_scales(recv2.at[t]) for t in range(last)]
    for c in range(CS):
        value = own[last, c]
        for t in range(last):
            value = value + decode(c, scales[t], recv2.at[t])
        out_ref[c] = value.astype(jnp.bfloat16)

    for copy in gathers:
        copy.wait_send()

    def finish(t, _):
        for j in range(1, PLANE):
            copy1(t, j).wait_send()
        return 0

    lax.fori_loop(0, planes, finish, 0)
    for t in range(last):
        copy2(t).wait_send()


def per_device(x_blocks, pair_left, pair_right, pair_target):
    n = lax.axis_size("blk")
    g = lax.axis_size("grp")
    nb, bs = x_blocks.shape[0], x_blocks.shape[1]
    pairs = pair_left.shape[3]
    planes = n // PLANE
    message = CS * bs + 16
    vmem = pl.BlockSpec(memory_space=pltpu.VMEM)
    smem = pl.BlockSpec(memory_space=pltpu.SMEM)
    dma = pltpu.SemaphoreType.DMA
    out = pl.pallas_call(
        functools.partial(kernel, n, g, nb, bs, pairs),
        out_shape=jax.ShapeDtypeStruct((CS, bs, bs), jnp.bfloat16),
        in_specs=[vmem, smem, smem, smem],
        out_specs=vmem,
        scratch_shapes=[
            pltpu.VMEM((g * nb, bs, bs), jnp.bfloat16),
            pltpu.VMEM((g * nb, bs, bs), jnp.bfloat16),
            pltpu.VMEM((pairs, bs, bs), jnp.float32),
            pltpu.VMEM((CS, bs, bs), jnp.float32),
            pltpu.VMEM((planes, CS, bs, bs), jnp.float32),
            pltpu.VMEM((planes, PLANE - 1, message, bs), jnp.int16),
            pltpu.VMEM((planes, PLANE - 1, message, bs), jnp.int16),
            pltpu.VMEM((planes - 1, message, bs), jnp.int16),
            pltpu.VMEM((planes - 1, message, bs), jnp.int16),
            dma((g - 1,)),
            dma((g - 1,)),
            dma((planes, PLANE - 1)),
            dma((planes, PLANE - 1)),
            dma((planes - 1,)),
            dma((planes - 1,)),
        ],
        compiler_params=pltpu.CompilerParams(
            collective_id=0, has_side_effects=True, vmem_limit_bytes=48 * 1024 * 1024
        ),
    )(x_blocks, pair_left[0, 0], pair_right[0, 0], pair_target[0, 0])
    return out.reshape(1, 1, CS, bs, bs)


def solution(mesh):
    return jax.shard_map(
        per_device,
        mesh=mesh,
        in_specs=(
            P(("blk", "grp"), None, None),
            P("blk", "grp", None, None),
            P("blk", "grp", None, None),
            P("blk", "grp", None, None),
        ),
        out_specs=P("blk", "grp", None, None, None),
        check_vma=False,
    )
```

time: 209 us -> 40.1 us (0.19)
  waiting for transfers between devices: 151 us -> 0 us
  Pallas kernels: 0 us -> 36.5 us
  matrix products: 26.5 us -> 0 us
  between operations: 13.4 us -> 0.01 us
  local copies, waits for them, and re-layouts: 12.4 us -> 3.25 us
  starting transfers between devices: 2.59 us -> 0 us
    ppermute x15 -> x0, waiting for transfers between devices: 142 us -> none  [from_behind(): return lax.ppermute(block, axis, route)]
    pallas_call x0 -> x1, Pallas kernels: none -> 36.5 us  [per_device(): pl.pallas_call(functools.partial(kernel, n, g, nb, bs, pairs), out_shape=...]
    dot_general x48 -> x0, matrix products: 26.5 us -> none  [the longest x16 14.5 us: partial_value(): jnp.einsum('pc,pyz->cyz', selector, product, precision=lax.Precision.HIGH...]
    all_gather x1 -> x0, waiting for transfers between devices: 8.79 us -> none  [per_device(): gathered = lax.all_gather(x_blocks, 'grp', axis=0, tiled=True)]
    while x31 -> x0, local copies, waits for them, and re-layouts: 3.42 us -> none
    ppermute x15 -> x0, starting transfers between devices: 2.59 us -> none  [from_behind(): return lax.ppermute(block, axis, route)]
    dynamic_slice x2 -> x0, local copies, waits for them, and re-layouts: 2.24 us -> none  [the longest x1 1.23 us: partial_value(): lax.dynamic_index_in_dim(right_all, turn_index, 0, keepdims=False)]
    unnamed x8 -> x10, local copies, waits for them, and re-layouts: 4.48 us -> 3.25 us
  transfers between devices with their start and end apart: 16 -> 0, of which waited for: 16 -> 0; matrix products, arithmetic and copies ran while one was open for 10% -> 0% of each run, Pallas kernels for 0% -> 0%
where the time goes in v1:
time: 40.1 us; the launch traced here: 39.8 us
  Pallas kernels  36.5 us (91%)
  local copies, waits for them, and re-layouts  3.25 us (8%)
    pallas_call x1, Pallas kernels, per_device(): pl.pallas_call(functools.partial(kernel, n, g, nb, bs, pairs), out_shape=...  36.5 us
    unnamed x10, local copies, waits for them, and re-layouts  3.25 us

profile of v1, /device:TPU:0, one launch (start us, length us, event | category | flops | bytes accessed | tf_op | source)
XLA Modules:
  0.0 39.8 jit_solution(1043084655620671819)
XLA Ops:
  0.0 0.0 copy-start.1
  0.0 0.8 %copy.5 = s32[1,1,16,12]{3,2,1,0:T(8,128)S(1)} copy(s32[1,1,16,12]{2,1,3,0:T(1,128)} %param.5) | data formatting | bytes 1536 | tf_op args[1]
  0.8 0.0 copy-done.1
  0.8 0.0 copy-start.2
  0.8 0.1 copy.6
  0.9 0.6 %copy-done.2 = s32[1,1,16,12]{2,1,3,0:T(1,128)S(1)} copy-done((s32[1,1,16,12]{2,1,3,0:T(1,128)S(1)}, s32[1,1,16,12]{2,1,3,0:T(1,128)}, u32[]{:S(2)}) %copy-start.2) | copy-done | bytes 792
  1.5 0.1 copy.7
  1.6 0.0 copy-start
  1.6 1.0 %copy-done = bf16[16,128,128]{2,1,0:T(8,128)(2,1)S(1)} copy-done((bf16[16,128,128]{2,1,0:T(8,128)(2,1)S(1)}, bf16[16,128,128]{2,1,0:T(8,128)(2,1)}, u32[]{:S(2)}) %copy-start) | copy-done | bytes 524312
  2.6 36.5 %shard_map.46 = bf16[4,128,128]{2,1,0:T(8,128)(2,1)S(1)} custom-call(bf16[16,128,128]{2,1,0:T(8,128)(2,1)S(1)} %copy-done, s32[16,12]{1,0:T(8,128)S(1)} %bitcast.5, s32[16,12]{1,0:T(8,128)S(1)} %bitcast.6, s32[16,12]{1,0:T(8,128)S(1)} %bitcast.7), custom_call_target="tpu_custom_call" | custom-call | tf_op jit(solution)/shard_map/pallas_call | solution.py:226
  39.2 0.7 %copy.9 = bf16[1,1,4,128,128]{4,3,2,1,0:T(8,128)(2,1)} copy(bf16[1,1,4,128,128]{4,3,2,1,0:T(8,128)(2,1)S(1)} %bitcast.4) | data formatting | bytes 262144
Async XLA Ops:
  0.0 0.8 %copy-start.1 = (s32[1,1,16,12]{2,1,3,0:T(1,128)S(1)}, s32[1,1,16,12]{2,1,3,0:T(1,128)}, u32[]{:S(2)}) copy-start(s32[1,1,16,12]{2,1,3,0:T(1,128)} %param.6) | copy-start | bytes 2308
  0.8 0.7 %copy-start.2 = (s32[1,1,16,12]{2,1,3,0:T(1,128)S(1)}, s32[1,1,16,12]{2,1,3,0:T(1,128)}, u32[]{:S(2)}) copy-start(s32[1,1,16,12]{2,1,3,0:T(1,128)} %param.7) | copy-start | bytes 2308
  1.6 1.0 %copy-start = (bf16[16,128,128]{2,1,0:T(8,128)(2,1)S(1)}, bf16[16,128,128]{2,1,0:T(8,128)(2,1)}, u32[]{:S(2)}) copy-start(bf16[16,128,128]{2,1,0:T(8,128)(2,1)} %x_ref.1) | copy-start | bytes 1572868

commit v2 on v1

v2 whole, which is shorter than its diff:
```python
import functools

import jax
import jax.numpy as jnp
from jax import lax
from jax.experimental import pallas as pl
from jax.experimental.pallas import tpu as pltpu
from jax.sharding import PartitionSpec as P

CS = 4
PLANE = 4
HALF = CS // 2
STEPS = 32700.0
FINE = 64.0
MESH = pl.DeviceIdType.MESH


def kernel(
    n, g, nb, bs, pairs,
    x_ref, left_ref, right_ref, target_ref, out_ref,
    panel, panel_t, prods, acc, send_a, recv_a, send_b, recv_b, send2, recv2,
    gather_send, gather_recv, sem_sa, sem_ra, sem_sb, sem_rb, sem_s2, sem_r2,
):
    planes = n // PLANE
    me = lax.axis_index("blk")
    q = lax.axis_index("grp")
    hi, lo = me // PLANE, me % PLANE

    def far(k):
        return (hi ^ k) * PLANE + lo

    def near(j):
        return hi * PLANE + (lo ^ j)

    barrier = pltpu.get_barrier_semaphore()
    for d in range(1, g):
        pl.semaphore_signal(barrier, inc=1, device_id=(me, (q + d) % g), device_id_type=MESH)
    for j in (1, 2):
        pl.semaphore_signal(barrier, inc=1, device_id=(near(j), q), device_id_type=MESH)
    for k in range(1, planes):
        pl.semaphore_signal(barrier, inc=1, device_id=(far(k), q), device_id_type=MESH)
    pl.semaphore_wait(barrier, (g - 1) + 2 + (planes - 1))

    gathers = []
    for d in range(1, g):
        copy = pltpu.make_async_remote_copy(
            src_ref=x_ref,
            dst_ref=panel.at[pl.ds(q * nb, nb)],
            send_sem=gather_send.at[d - 1],
            recv_sem=gather_recv.at[d - 1],
            device_id=(me, (q + d) % g),
            device_id_type=MESH,
        )
        copy.start()
        gathers.append(copy)

    def take_own(i, _):
        block = x_ref[i]
        panel[q * nb + i] = block
        panel_t[q * nb + i] = block.T
        return 0

    lax.fori_loop(0, nb, take_own, 0)
    for d in range(1, g):
        gathers[d - 1].wait_recv()
        source = (q - d + g) % g

        def take_other(i, _):
            panel_t[source * nb + i] = panel[source * nb + i].T
            return 0

        lax.fori_loop(0, nb, take_other, 0)

    def partial_sum(t, m):
        owner = (hi ^ ((t + 1) % planes)) * PLANE + (lo ^ m)
        s = (me - 1 - owner + 2 * n) % n
        for p in range(pairs):
            prods[p] = jnp.dot(
                panel_t[left_ref[s, p]],
                panel[right_ref[s, p]],
                preferred_element_type=jnp.float32,
            )
        masks = [
            [jnp.where(target_ref[s, p] == c, 1.0, 0.0) for c in range(CS)] for p in range(pairs)
        ]
        strip = 16
        for i in range(bs // strip):
            rows = pl.ds(i * strip, strip)
            totals = [None] * CS
            for p in range(pairs):
                value = prods[p, rows, :]
                for c in range(CS):
                    term = value * masks[p][c]
                    totals[c] = term if totals[c] is None else totals[c] + term
            for c in range(CS):
                acc[t, m, c, rows, :] = totals[c]

    def encode(values, dst):
        row = lax.broadcasted_iota(jnp.int32, (16, bs), 0)
        table = jnp.zeros((16, bs), jnp.float32)
        for i, value in enumerate(values):
            most = jnp.max(jnp.abs(value), axis=0, keepdims=True)
            level = jnp.ceil(jnp.log(jnp.maximum(most, 1e-30)) * FINE) + 1.0
            inverse = jnp.exp(level * (-1.0 / FINE)) * STEPS
            coded = jnp.round(value * inverse).astype(jnp.int32).astype(jnp.int16)
            dst[pl.ds(i * bs, bs), :] = coded
            table = jnp.where(row == i, level, table)
        dst[pl.ds(len(values) * bs, 16), :] = table.astype(jnp.int32).astype(jnp.int16)

    def decode(count, src):
        level = src[pl.ds(count * bs, 16), :].astype(jnp.int32).astype(jnp.float32)
        scales = jnp.exp(level * (1.0 / FINE)) * (1.0 / STEPS)

        def block(i):
            value = src[pl.ds(i * bs, bs), :].astype(jnp.int32).astype(jnp.float32)
            return value * scales[i : i + 1, :]

        return block

    def copy_a(t, h, a):
        return pltpu.make_async_remote_copy(
            src_ref=send_a.at[t, h, a],
            dst_ref=recv_a.at[t, h, a],
            send_sem=sem_sa.at[t, h, a],
            recv_sem=sem_ra.at[t, h, a],
            device_id=(near(1 + h), q),
            device_id_type=MESH,
        )

    def copy_b(t, h):
        return pltpu.make_async_remote_copy(
            src_ref=send_b.at[t, h],
            dst_ref=recv_b.at[t, h],
            send_sem=sem_sb.at[t, h],
            recv_sem=sem_rb.at[t, h],
            device_id=(near(2 - h), q),
            device_id_type=MESH,
        )

    def copy2(t):
        return pltpu.make_async_remote_copy(
            src_ref=send2.at[t],
            dst_ref=recv2.at[t],
            send_sem=sem_s2.at[t],
            recv_sem=sem_r2.at[t],
            device_id=(far(t + 1), q),
            device_id_type=MESH,
        )

    def compute(t):
        def one(j, _):
            m = PLANE - 1 - j
            partial_sum(t, m)

            def send(h, a):
                encode([acc[t, m, HALF * h + i] for i in range(HALF)], send_a.at[t, h, a])
                copy_a(t, h, a).start()

            @pl.when(m == PLANE - 1)
            def _():
                for h in range(2):
                    send(h, 0)

            @pl.when((m == 1) | (m == 2))
            def _():
                send(m - 1, 1)

            return 0

        lax.fori_loop(0, PLANE, one, 0)

    def turn_corner(t):
        for h in range(2):
            copy_a(t, h, 0).wait_recv()
            came = decode(HALF, recv_a.at[t, h, 0])
            encode(
                [acc[t, 2 - h, HALF * h + i] + came(i) for i in range(HALF)], send_b.at[t, h]
            )
            copy_b(t, h).start()

    def plane_total(t):
        for h in range(2):
            copy_a(t, h, 1).wait_recv()
            copy_b(t, h).wait_recv()
            first = decode(HALF, recv_a.at[t, h, 1])
            second = decode(HALF, recv_b.at[t, h])
            for i in range(HALF):
                acc[t, 0, HALF * h + i] = acc[t, 0, HALF * h + i] + first(i) + second(i)

    def pass_on(t):
        plane_total(t)
        encode([acc[t, 0, c] for c in range(CS)], send2.at[t])
        copy2(t).start()

    last = planes - 1

    def turn(t, _):
        @pl.when(t < planes)
        def _():
            compute(t)

        @pl.when((t >= 1) & (t < planes + 1))
        def _():
            turn_corner(t - 1)

        @pl.when(t >= 2)
        def _():
            pass_on(t - 2)

        return 0

    lax.fori_loop(0, last + 2, turn, 0)

    plane_total(last)
    for t in range(last):
        copy2(t).wait_recv()
    came = [decode(CS, recv2.at[t]) for t in range(last)]
    for c in range(CS):
        value = acc[last, 0, c]
        for t in range(last):
            value = value + came[t](c)
        out_ref[c] = value.astype(jnp.bfloat16)

    for copy in gathers:
        copy.wait_send()

    def finish(t, _):
        for h in range(2):
            for a in range(2):
                copy_a(t, h, a).wait_send()
            copy_b(t, h).wait_send()
        return 0

    lax.fori_loop(0, planes, finish, 0)
    for t in range(last):
        copy2(t).wait_send()


def per_device(x_blocks, pair_left, pair_right, pair_target):
    n = lax.axis_size("blk")
    g = lax.axis_size("grp")
    nb, bs = x_blocks.shape[0], x_blocks.shape[1]
    pairs = pair_left.shape[3]
    planes = n // PLANE
    message = CS * bs + 16
    short = HALF * bs + 16
    vmem = pl.BlockSpec(memory_space=pltpu.VMEM)
    smem = pl.BlockSpec(memory_space=pltpu.SMEM)
    dma = pltpu.SemaphoreType.DMA
    out = pl.pallas_call(
        functools.partial(kernel, n, g, nb, bs, pairs),
        out_shape=jax.ShapeDtypeStruct((CS, bs, bs), jnp.bfloat16),
        in_specs=[vmem, smem, smem, smem],
        out_specs=vmem,
        scratch_shapes=[
            pltpu.VMEM((g * nb, bs, bs), jnp.bfloat16),
            pltpu.VMEM((g * nb, bs, bs), jnp.bfloat16),
            pltpu.VMEM((pairs, bs, bs), jnp.float32),
            pltpu.VMEM((planes, PLANE, CS, bs, bs), jnp.float32),
            pltpu.VMEM((planes, 2, 2, short, bs), jnp.int16),
            pltpu.VMEM((planes, 2, 2, short, bs), jnp.int16),
            pltpu.VMEM((planes, 2, short, bs), jnp.int16),
            pltpu.VMEM((planes, 2, short, bs), jnp.int16),
            pltpu.VMEM((planes - 1, message, bs), jnp.int16),
            pltpu.VMEM((planes - 1, message, bs), jnp.int16),
            dma((g - 1,)),
            dma((g - 1,)),
            dma((planes, 2, 2)),
            dma((planes, 2, 2)),
            dma((planes, 2)),
            dma((planes, 2)),
            dma((planes - 1,)),
            dma((planes - 1,)),
        ],
        compiler_params=pltpu.CompilerParams(
            collective_id=0, has_side_effects=True, vmem_limit_bytes=48 * 1024 * 1024
        ),
    )(x_blocks, pair_left[0, 0], pair_right[0, 0], pair_target[0, 0])
    return out.reshape(1, 1, CS, bs, bs)


def solution(mesh):
    return jax.shard_map(
        per_device,
        mesh=mesh,
        in_specs=(
            P(("blk", "grp"), None, None),
            P("blk", "grp", None, None),
            P("blk", "grp", None, None),
            P("blk", "grp", None, None),
        ),
        out_specs=P("blk", "grp", None, None, None),
        check_vma=False,
    )
```

time: 40.1 us -> 38.9 us (0.970)
  Pallas kernels: 36.5 us -> 35.2 us
    pallas_call x1, Pallas kernels: 36.5 us -> 35.2 us  [per_device(): pl.pallas_call(functools.partial(kernel, n, g, nb, bs, pairs), out_shape=...]
where the time goes in v2:
time: 38.9 us; the launch traced here: 38.5 us
  Pallas kernels  35.2 us (90%)
  local copies, waits for them, and re-layouts  3.25 us (8%)
    pallas_call x1, Pallas kernels, per_device(): pl.pallas_call(functools.partial(kernel, n, g, nb, bs, pairs), out_shape=...  35.2 us
    unnamed x10, local copies, waits for them, and re-layouts  3.25 us

profile of v2, /device:TPU:0, one launch (start us, length us, event | category | flops | bytes accessed | tf_op | source)
XLA Modules:
  0.0 38.5 jit_solution(7617796249041297957)
XLA Ops:
  0.0 0.0 copy-start.1
  0.0 0.8 %copy.5 = s32[1,1,16,12]{3,2,1,0:T(8,128)S(1)} copy(s32[1,1,16,12]{2,1,3,0:T(1,128)} %param.5) | data formatting | bytes 1536 | tf_op args[1]
  0.8 0.0 copy-done.1
  0.8 0.0 copy-start.2
  0.8 0.1 copy.6
  0.9 0.6 %copy-done.2 = s32[1,1,16,12]{2,1,3,0:T(1,128)S(1)} copy-done((s32[1,1,16,12]{2,1,3,0:T(1,128)S(1)}, s32[1,1,16,12]{2,1,3,0:T(1,128)}, u32[]{:S(2)}) %copy-start.2) | copy-done | bytes 792
  1.5 0.1 copy.7
  1.6 0.0 copy-start
  1.6 1.0 %copy-done = bf16[16,128,128]{2,1,0:T(8,128)(2,1)S(1)} copy-done((bf16[16,128,128]{2,1,0:T(8,128)(2,1)S(1)}, bf16[16,128,128]{2,1,0:T(8,128)(2,1)}, u32[]{:S(2)}) %copy-start) | copy-done | bytes 524312
  2.6 35.2 %shard_map.46 = bf16[4,128,128]{2,1,0:T(8,128)(2,1)S(1)} custom-call(bf16[16,128,128]{2,1,0:T(8,128)(2,1)S(1)} %copy-done, s32[16,12]{1,0:T(8,128)S(1)} %bitcast.5, s32[16,12]{1,0:T(8,128)S(1)} %bitcast.6, s32[16,12]{1,0:T(8,128)S(1)} %bitcast.7), custom_call_target="tpu_custom_call" | custom-call | tf_op jit(solution)/shard_map/pallas_call | solution.py:250
  37.8 0.7 %copy.9 = bf16[1,1,4,128,128]{4,3,2,1,0:T(8,128)(2,1)} copy(bf16[1,1,4,128,128]{4,3,2,1,0:T(8,128)(2,1)S(1)} %bitcast.4) | data formatting | bytes 262144
Async XLA Ops:
  0.0 0.8 %copy-start.1 = (s32[1,1,16,12]{2,1,3,0:T(1,128)S(1)}, s32[1,1,16,12]{2,1,3,0:T(1,128)}, u32[]{:S(2)}) copy-start(s32[1,1,16,12]{2,1,3,0:T(1,128)} %param.6) | copy-start | bytes 2308
  0.8 0.7 %copy-start.2 = (s32[1,1,16,12]{2,1,3,0:T(1,128)S(1)}, s32[1,1,16,12]{2,1,3,0:T(1,128)}, u32[]{:S(2)}) copy-start(s32[1,1,16,12]{2,1,3,0:T(1,128)} %param.7) | copy-start | bytes 2308
  1.6 1.0 %copy-start = (bf16[16,128,128]{2,1,0:T(8,128)(2,1)S(1)}, bf16[16,128,128]{2,1,0:T(8,128)(2,1)}, u32[]{:S(2)}) copy-start(bf16[16,128,128]{2,1,0:T(8,128)(2,1)} %x_ref.1) | copy-start | bytes 1572868

commit v3 on v2

--- a/solution.py
+++ b/solution.py
@@ -19,7 +19,7 @@
     n, g, nb, bs, pairs,
     x_ref, left_ref, right_ref, target_ref, out_ref,
     panel, panel_t, prods, acc, send_a, recv_a, send_b, recv_b, send2, recv2,
-    gather_send, gather_recv, sem_sa, sem_ra, sem_sb, sem_rb, sem_s2, sem_r2,
+    gather_own, gather_send, gather_recv, sem_sa, sem_ra, sem_sb, sem_rb, sem_s2, sem_r2,
 ):
     planes = n // PLANE
     me = lax.axis_index("blk")
@@ -32,6 +32,8 @@
     def near(j):
         return hi * PLANE + (lo ^ j)
 
+    held = pltpu.make_async_copy(x_ref, panel.at[pl.ds(q * nb, nb)], gather_own)
+    held.start()
     barrier = pltpu.get_barrier_semaphore()
     for d in range(1, g):
         pl.semaphore_signal(barrier, inc=1, device_id=(me, (q + d) % g), device_id_type=MESH)
@@ -55,11 +57,10 @@
         gathers.append(copy)
 
     def take_own(i, _):
-        block = x_ref[i]
-        panel[q * nb + i] = block
-        panel_t[q * nb + i] = block.T
+        panel_t[q * nb + i] = panel[q * nb + i].T
         return 0
 
+    held.wait()
     lax.fori_loop(0, nb, take_own, 0)
     for d in range(1, g):
         gathers[d - 1].wait_recv()
@@ -72,16 +73,16 @@
         lax.fori_loop(0, nb, take_other, 0)
 
     def partial_sum(t, m):
-        owner = (hi ^ ((t + 1) % planes)) * PLANE + (lo ^ m)
+        owner = (hi ^ (planes - 1 - t)) * PLANE + (lo ^ m)
         s = (me - 1 - owner + 2 * n) % n
         for p in range(pairs):
             prods[p] = jnp.dot(
-                panel_t[left_ref[s, p]],
-                panel[right_ref[s, p]],
+                panel_t[left_ref[p, 0, s]],
+                panel[right_ref[p, 0, s]],
                 preferred_element_type=jnp.float32,
             )
         masks = [
-            [jnp.where(target_ref[s, p] == c, 1.0, 0.0) for c in range(CS)] for p in range(pairs)
+            [jnp.where(target_ref[p, 0, s] == c, 1.0, 0.0) for c in range(CS)] for p in range(pairs)
         ]
         strip = 16
         for i in range(bs // strip):
@@ -143,11 +144,11 @@
             dst_ref=recv2.at[t],
             send_sem=sem_s2.at[t],
             recv_sem=sem_r2.at[t],
-            device_id=(far(t + 1), q),
+            device_id=(far(planes - 1 - t), q),
             device_id_type=MESH,
         )
 
-    def compute(t):
+    def compute(t, begin, end):
         def one(j, _):
             m = PLANE - 1 - j
             partial_sum(t, m)
@@ -167,7 +168,7 @@
 
             return 0
 
-        lax.fori_loop(0, PLANE, one, 0)
+        lax.fori_loop(begin, end, one, 0)
 
     def turn_corner(t):
         for h in range(2):
@@ -197,11 +198,15 @@
     def turn(t, _):
         @pl.when(t < planes)
         def _():
-            compute(t)
+            compute(t, 0, 1)
 
         @pl.when((t >= 1) & (t < planes + 1))
         def _():
             turn_corner(t - 1)
+
+        @pl.when(t < planes)
+        def _():
+            compute(t, 1, PLANE)
 
         @pl.when(t >= 2)
         def _():
@@ -247,10 +252,11 @@
     vmem = pl.BlockSpec(memory_space=pltpu.VMEM)
     smem = pl.BlockSpec(memory_space=pltpu.SMEM)
     dma = pltpu.SemaphoreType.DMA
+    tables = [jnp.transpose(a[0], (2, 0, 1)) for a in (pair_left, pair_right, pair_target)]
     out = pl.pallas_call(
         functools.partial(kernel, n, g, nb, bs, pairs),
         out_shape=jax.ShapeDtypeStruct((CS, bs, bs), jnp.bfloat16),
-        in_specs=[vmem, smem, smem, smem],
+        in_specs=[pl.BlockSpec(memory_space=pltpu.HBM), smem, smem, smem],
         out_specs=vmem,
         scratch_shapes=[
             pltpu.VMEM((g * nb, bs, bs), jnp.bfloat16),
@@ -263,6 +269,7 @@
             pltpu.VMEM((planes, 2, short, bs), jnp.int16),
             pltpu.VMEM((planes - 1, message, bs), jnp.int16),
             pltpu.VMEM((planes - 1, message, bs), jnp.int16),
+            dma,
             dma((g - 1,)),
             dma((g - 1,)),
             dma((planes, 2, 2)),
@@ -273,9 +280,9 @@
             dma((planes - 1,)),
         ],
         compiler_params=pltpu.CompilerParams(
-            collective_id=0, has_side_effects=True, vmem_limit_bytes=48 * 1024 * 1024
+            collective_id=0, has_side_effects=True, vmem_limit_bytes=64 * 1024 * 1024
         ),
-    )(x_blocks, pair_left[0, 0], pair_right[0, 0], pair_target[0, 0])
+    )(x_blocks, *tables)
     return out.reshape(1, 1, CS, bs, bs)
 
 

time: 38.9 us -> 37.2 us (0.956)
  local copies, waits for them, and re-layouts: 3.25 us -> 1.57 us
    unnamed x10 -> x1, local copies, waits for them, and re-layouts: 3.25 us -> 1.57 us
where the time goes in v3:
time: 37.2 us; the launch traced here: 37 us
  Pallas kernels  35.4 us (95%)
  local copies, waits for them, and re-layouts  1.57 us (4%)
    pallas_call x1, Pallas kernels, per_device(): pl.pallas_call(functools.partial(kernel, n, g, nb, bs, pairs), out_shape=...  35.4 us
    unnamed x1, local copies, waits for them, and re-layouts  1.57 us

profile of v3, /device:TPU:0, one launch (start us, length us, event | category | flops | bytes accessed | tf_op | source)
XLA Modules:
  0.0 37.0 jit_solution(10715231896611131787)
XLA Ops:
  0.0 35.4 %shard_map.46 = bf16[4,128,128]{2,1,0:T(8,128)(2,1)} custom-call(bf16[16,128,128]{2,1,0:T(8,128)(2,1)} %x_ref.1, s32[12,1,16]{2,1,0:T(1,128)} %bitcast.11, s32[12,1,16]{2,1,0:T(1,128)} %bitcast.12, s32[12,1,16]{2,1,0:T(1,128)} %bitcast.13), custom_call_target="tpu_custom_call" | custom-call | tf_op jit(solution)/shard_map/pallas_call | solution.py:256
  35.4 1.6 %copy.6 = bf16[1,1,4,128,128]{4,3,2,1,0:T(8,128)(2,1)} copy(bf16[1,1,4,128,128]{4,3,2,1,0:T(8,128)(2,1)} %bitcast.10) | data formatting | bytes 262144

commit v4 on v3

--- a/solution.py
+++ b/solution.py
@@ -9,6 +9,7 @@
 
 CS = 4
 PLANE = 4
+BESIDE = 1
 HALF = CS // 2
 STEPS = 32700.0
 FINE = 64.0
@@ -72,8 +73,14 @@
 
         lax.fori_loop(0, nb, take_other, 0)
 
+    last = planes - 1
+
+    def plane_of(t):
+        inner = jnp.where(t == BESIDE, 1, planes - t - jnp.where(t == 0, 1, 0))
+        return jnp.where(t == last, 0, inner)
+
     def partial_sum(t, m):
-        owner = (hi ^ (planes - 1 - t)) * PLANE + (lo ^ m)
+        owner = (hi ^ plane_of(t)) * PLANE + (lo ^ m)
         s = (me - 1 - owner + 2 * n) % n
         for p in range(pairs):
             prods[p] = jnp.dot(
@@ -124,7 +131,7 @@
             dst_ref=recv_a.at[t, h, a],
             send_sem=sem_sa.at[t, h, a],
             recv_sem=sem_ra.at[t, h, a],
-            device_id=(near(1 + h), q),
+            device_id=(jnp.where(t == BESIDE, far(1), near(1 + h)), q),
             device_id_type=MESH,
         )
 
@@ -144,7 +151,7 @@
             dst_ref=recv2.at[t],
             send_sem=sem_s2.at[t],
             recv_sem=sem_r2.at[t],
-            device_id=(far(planes - 1 - t), q),
+            device_id=(far(plane_of(t)), q),
             device_id_type=MESH,
         )
 
@@ -154,6 +161,13 @@
             partial_sum(t, m)
 
             def send(h, a):
+                @pl.when(t == last)
+                def _():
+                    copy_a(BESIDE, h, a).wait_recv()
+                    came = decode(HALF, recv_a.at[BESIDE, h, a])
+                    for i in range(HALF):
+                        acc[t, m, HALF * h + i] = acc[t, m, HALF * h + i] + came(i)
+
                 encode([acc[t, m, HALF * h + i] for i in range(HALF)], send_a.at[t, h, a])
                 copy_a(t, h, a).start()
 
@@ -172,28 +186,34 @@
 
     def turn_corner(t):
         for h in range(2):
-            copy_a(t, h, 0).wait_recv()
-            came = decode(HALF, recv_a.at[t, h, 0])
-            encode(
-                [acc[t, 2 - h, HALF * h + i] + came(i) for i in range(HALF)], send_b.at[t, h]
-            )
+            @pl.when(t != BESIDE)
+            def _():
+                copy_a(t, h, 0).wait_recv()
+                came = decode(HALF, recv_a.at[t, h, 0])
+                for i in range(HALF):
+                    acc[t, 2 - h, HALF * h + i] = acc[t, 2 - h, HALF * h + i] + came(i)
+
+            encode([acc[t, 2 - h, HALF * h + i] for i in range(HALF)], send_b.at[t, h])
             copy_b(t, h).start()
 
     def plane_total(t):
         for h in range(2):
-            copy_a(t, h, 1).wait_recv()
+            @pl.when(t != BESIDE)
+            def _():
+                copy_a(t, h, 1).wait_recv()
+                first = decode(HALF, recv_a.at[t, h, 1])
+                for i in range(HALF):
+                    acc[t, 0, HALF * h + i] = acc[t, 0, HALF * h + i] + first(i)
+
             copy_b(t, h).wait_recv()
-            first = decode(HALF, recv_a.at[t, h, 1])
             second = decode(HALF, recv_b.at[t, h])
             for i in range(HALF):
-                acc[t, 0, HALF * h + i] = acc[t, 0, HALF * h + i] + first(i) + second(i)
+                acc[t, 0, HALF * h + i] = acc[t, 0, HALF * h + i] + second(i)
 
     def pass_on(t):
         plane_total(t)
         encode([acc[t, 0, c] for c in range(CS)], send2.at[t])
         copy2(t).start()
-
-    last = planes - 1
 
     def turn(t, _):
         @pl.when(t < planes)

time: 37.2 us -> 35.2 us (0.946)
  Pallas kernels: 35.4 us -> 33.4 us
    pallas_call x1, Pallas kernels: 35.4 us -> 33.4 us  [per_device(): pl.pallas_call(functools.partial(kernel, n, g, nb, bs, pairs), out_shape=...]
where the time goes in v4:
time: 35.2 us; the launch traced here: 35 us
  Pallas kernels  33.4 us (95%)
  local copies, waits for them, and re-layouts  1.57 us (4%)
    pallas_call x1, Pallas kernels, per_device(): pl.pallas_call(functools.partial(kernel, n, g, nb, bs, pairs), out_shape=...  33.4 us
    unnamed x1, local copies, waits for them, and re-layouts  1.57 us

profile of v4, /device:TPU:0, one launch (start us, length us, event | category | flops | bytes accessed | tf_op | source)
XLA Modules:
  0.0 35.0 jit_solution(2130246811652901575)
XLA Ops:
  0.0 33.4 %shard_map.46 = bf16[4,128,128]{2,1,0:T(8,128)(2,1)} custom-call(bf16[16,128,128]{2,1,0:T(8,128)(2,1)} %x_ref.1, s32[12,1,16]{2,1,0:T(1,128)} %bitcast.11, s32[12,1,16]{2,1,0:T(1,128)} %bitcast.12, s32[12,1,16]{2,1,0:T(1,128)} %bitcast.13), custom_call_target="tpu_custom_call" | custom-call | tf_op jit(solution)/shard_map/pallas_call | solution.py:276
  33.4 1.6 %copy.6 = bf16[1,1,4,128,128]{4,3,2,1,0:T(8,128)(2,1)} copy(bf16[1,1,4,128,128]{4,3,2,1,0:T(8,128)(2,1)} %bitcast.10) | data formatting | bytes 262144
